TPU v7x, 32 devices: a whole 2x2x4 slice. The times are simulated.
32 devices in a mesh: tm: 8 (over z, x), feat: 4 (over y, core).
Axes of the slice: x: 2, y: 2, z: 4, core: 2. Of those that a mesh axis runs over, the one named last changes fastest.
Arguments:
- activations: bfloat16 [20480, 2048], P(('tm', 'feat')), may hold values from -19 to 19
- targets: bfloat16 [20480, 128], P(('tm', 'feat')), may hold values from -8 to 8
- span_of: int32 [20480], P(('tm', 'feat')), may hold values from 0 to 7, as said below
Outputs:
- predictions: bfloat16 [20480, 128], P(('tm', 'feat'))
- surprise: float32 [20480], P(('tm', 'feat'))
Inputs may be any that keep to these rules, and one draw needn't show every extreme that they name: `span_of`: in each aligned block of 640 rows (the rows of one device) every span from 0 to 7 appears exactly 80 times.
All inputs are finite; a program needn't handle non-finite values.
Results may differ from a plain program's by a relative error of at most 0.0049.
Values may be sent and summed in bfloat16 or wider, within the bound.
A program may use at most 320 MiB of HBM per device.

v0:
```python
import jax
import jax.numpy as jnp
from jax import lax
from jax.sharding import PartitionSpec as P

ITERS = 3


RIDGE = 0.1
TINY = 1e-06


def carried_in(shard, axis, combine, identity):
    length, position = (lax.axis_size(axis), lax.axis_index(axis))
    everything = jax.tree.map(lambda part: lax.all_gather(part, axis), shard)
    start = jax.tree.map(
        lambda part, zero: jnp.broadcast_to(jnp.asarray(zero, part.dtype), part.shape),
        shard,
        identity,
    )

    def hop(k, before):
        reached = k < position
        new = combine(before, jax.tree.map(lambda part: part[k], everything))
        return jax.tree.map(lambda a, b: jnp.where(reached, a, b), new, before)

    return lax.fori_loop(0, length, hop, start)


def body(activations, targets, span_of):
    spans = lax.axis_size("tm")
    feat_count = lax.axis_size("feat")
    tok_dev, width = activations.shape
    n_targets = targets.shape[1]
    block_rows = width // feat_count
    share = tok_dev // spans
    contract = (((0,), (0,)), ((), ()))
    highest = lax.Precision.HIGHEST
    order = jnp.argsort(span_of, stable=True)
    sorted_x = jnp.take(activations, order, axis=0).reshape(spans, share, width)
    sorted_y = jnp.take(targets, order, axis=0).reshape(spans, share, n_targets)
    moved_x, moved_y = (
        lax.all_to_all(sorted_x, "tm", split_axis=0, concat_axis=0, tiled=True),
        lax.all_to_all(sorted_y, "tm", split_axis=0, concat_axis=0, tiled=True),
    )
    local_x = moved_x.reshape(tok_dev, width)
    local_y = moved_y.reshape(tok_dev, n_targets)
    col_start = lax.axis_index("feat") * block_rows
    rows_x = lax.all_gather(local_x, "feat", axis=0, tiled=True)
    rows_y = lax.all_gather(local_y, "feat", axis=0, tiled=True)
    own = lax.dynamic_slice_in_dim(rows_x, col_start, block_rows, 1)
    gram_part = lax.dot_general(own, rows_x, contract, preferred_element_type=jnp.float32)
    cross_part = lax.dot_general(own, rows_y, contract, preferred_element_type=jnp.float32)

    def combine(earlier, later):
        return (earlier[0] + later[0], earlier[1] + later[1])

    identity = (jnp.zeros_like(gram_part), jnp.zeros_like(cross_part))
    gram_prefix, cross_prefix = carried_in((gram_part, cross_part), "tm", combine, identity)
    seen = (lax.axis_index("tm") * (tok_dev * feat_count)).astype(jnp.float32)
    scale = 1.0 / jnp.maximum(seen, 1.0)
    rhs = scale * cross_prefix

    def column_dot(left, right):
        return lax.psum(jnp.sum(left * right, axis=0), "feat")

    residual = rhs
    direction = rhs
    norm_now = column_dot(residual, residual)
    solution = None
    for step in range(ITERS):
        product = jnp.dot(
            gram_prefix,
            lax.all_gather(direction, "feat", axis=0, tiled=True),
            precision=highest,
            preferred_element_type=jnp.float32,
        )
        product, carried = (product, direction)
        image = scale * product + RIDGE * direction
        alpha = norm_now / (column_dot(direction, image) + TINY)
        update = alpha * carried
        solution = update if solution is None else solution + update
        if step + 1 < ITERS:
            residual = residual - alpha * image
            norm_next = column_dot(residual, residual)
            direction = residual + norm_next / (norm_now + TINY) * direction
            norm_now = norm_next
    weights = lax.all_gather(solution.astype(jnp.bfloat16), "feat", axis=0, tiled=True)
    predicted = jnp.dot(local_x, weights, preferred_element_type=jnp.float32).astype(jnp.bfloat16)
    returned = lax.all_to_all(
        predicted.reshape(spans, share, n_targets), "tm", split_axis=0, concat_axis=0, tiled=True
    )
    in_order = returned.reshape(tok_dev, n_targets)
    predictions = jnp.zeros_like(in_order).at[order].set(in_order)
    error = targets.astype(jnp.float32) - predictions.astype(jnp.float32)
    surprise = jnp.mean(error * error, axis=1)
    return (predictions, surprise)


def solution(mesh):
    return jax.shard_map(
        body,
        mesh=mesh,
        in_specs=(P(("tm", "feat"), None), P(("tm", "feat"), None), P(("tm", "feat"))),
        out_specs=(P(("tm", "feat"), None), P(("tm", "feat"))),
        check_vma=False,
    )
```

profile of v0, /device:TPU:0, one launch (start us, length us, event | category | flops | bytes accessed | tf_op | source)
XLA Modules:
  0.0 1048.4 jit_solution(16677421984998427793)
XLA Ops:
  7.2 0.0 all-gather.9.cloned.1.call-start
  7.2 5.2 sort.17
  12.5 0.1 broadcast_in_dim.43
  12.6 4.1 gather_fusion
  16.6 2.0 broadcast_select_fusion
  18.7 66.8 %all_to_all.15 = bf16[8,80,2048]{2,1,0:T(8,128)(2,1)} all-to-all(bf16[8,80,2048]{2,1,0:T(8,128)(2,1)S(1)} %broadcast_select_fusion), channel_id=1, replica_groups=mesh['tm'=8,'feat'=4] {'tm'}, dimensions={0} | all-to-all | bytes 5242880 | tf_op jit(solution)/shard_map/all_to_all | solution.py:43
  85.5 0.0 all-gather.9.cloned.1.call-update
  85.5 2.0 gather_fusion.1
  87.5 0.8 broadcast_select_fusion.1
  88.3 3.6 all-to-all-start.1
  91.9 0.0 all-gather.19.cloned.1.call-start
  92.0 7.5 all-to-all-done.1
  99.5 11.8 %all_gather.33 = bf16[2560,128]{1,0:T(8,128)(2,1)S(1)} all-gather(bf16[640,128]{1,0:T(8,128)(2,1)S(1)} %bitcast.31), channel_id=1, replica_groups=mesh['tm'=8,'feat'=4] {'feat'}, dimensions={0}, use_global_device_ids=true | all-gather | bytes 819200 | tf_op jit(solution)/shard_map/all_gather | solution.py:50
  111.3 47.1 %all-gather.9.cloned.1.call-done = bf16[2560,2048]{1,0:T(8,128)(2,1)} async-done(((bf16[640,2048]{1,0:T(8,128)(2,1)}), bf16[2560,2048]{1,0:T(8,128)(2,1)}) %all-gather.9.cloned.1.call-update) | async-done | bytes 10485776 | tf_op jit(solution)/shard_map/all_gather | solution.py:49
  158.4 3.3 fusion
  161.7 0.0 all-gather.19.cloned.1.call-update
  161.7 0.0 all-gather.17.cloned.1.call-start
  161.8 10.5 %fusion.2 = f32[512,2048]{1,0:T(8,128)} fusion(bf16[2560,2048]{1,0:T(8,128)(2,1)} %all-gather.9.cloned.1.call-done, s32[]{:T(128)S(6)} %select_n.61), kind=kOutput, calls=%fused_computation.8 | convolution fusion | flops 5368709120 | bytes 17301508 | tf_op jit(solution)/shard_map/dot_general | solution.py:52
  172.3 0.0 all-gather.17.cloned.1.call-update
  172.3 0.0 all-gather.11.cloned.1.call-start
  172.4 38.7 %all-gather.19.cloned.1.call-done = f32[4096,128]{1,0:T(8,128)} async-done(((f32[512,128]{1,0:T(8,128)}), f32[4096,128]{1,0:T(8,128)}) %all-gather.19.cloned.1.call-update) | async-done | bytes 2097168 | tf_op jit(solution)/shard_map/all_gather | solution.py:15
  211.2 637.8 %all-gather.17.cloned.1.call-done = f32[4096,2048]{1,0:T(8,128)} async-done(((f32[512,2048]{1,0:T(8,128)}), f32[4096,2048]{1,0:T(8,128)}) %all-gather.17.cloned.1.call-update) | async-done | bytes 33554448 | tf_op jit(solution)/shard_map/all_gather | solution.py:15
  849.0 60.9 %while.16 = (s32[]{:T(128)}, f32[512,2048]{1,0:T(8,128)}, f32[512,128]{1,0:T(8,128)S(1)}, s32[]{:T(128)}, f32[8,512,2048]{2,1,0:T(8,128)}, /*index=5*/f32[8,512,128]{2,1,0:T(8,128)}, s32[]{:T(128)}, s32[]{:T(128)}) while((s32[]{:T(128)}, f32[512,2048]{1,0:T(8,128)}, f32[512,128]{1,0:T(8,128)S(1)}, s32[]{:T(128)}, ...), condition=%wide.region_2.3_spmd.clone, body=%wide.region_1.2_spmd.clone.sunk | while | flops 3342340 | bytes 13369459 | solution.py:27
  849.0 5.4 add_select_fusion.4
  854.4 1.0 add_select_fusion.5
  855.5 6.7 add_select_fusion.4
  862.2 1.0 add_select_fusion.5
  863.2 6.7 add_select_fusion.4
  870.0 1.0 add_select_fusion.5
  871.0 6.7 add_select_fusion.4
  877.8 1.0 add_select_fusion.5
  878.8 6.7 add_select_fusion.4
  885.5 1.0 add_select_fusion.5
  886.6 6.7 add_select_fusion.4
  893.3 1.0 add_select_fusion.5
  894.4 6.7 add_select_fusion.4
  901.1 1.0 add_select_fusion.5
  902.1 6.7 add_select_fusion.4
  908.9 1.0 add_select_fusion.5
  909.9 0.7 broadcast_multiply_fusion
  910.7 0.0 all-gather.13.cloned.1.call-start
  910.7 16.8 %all-gather.11.cloned.1.call-done = f32[2048,128]{1,0:T(8,128)} async-done(((f32[512,128]{1,0:T(8,128)}), f32[2048,128]{1,0:T(8,128)}) %all-gather.11.cloned.1.call-update) | async-done | bytes 1048592 | tf_op jit(solution)/shard_map/all_gather | solution.py:74
  927.5 5.5 multiply_reduce_fusion.4
  933.0 5.9 all-reduce
  938.9 0.1 multiply_reduce_fusion.3
  939.0 5.7 psum.44
  944.7 0.8 multiply_add_fusion.1
  945.5 0.2 all-gather.15.cloned.1.call-start
  945.7 18.0 %all-gather.13.cloned.1.call-done = f32[2048,128]{1,0:T(8,128)} async-done(((f32[512,128]{1,0:T(8,128)}), f32[2048,128]{1,0:T(8,128)}) %all-gather.13.cloned.1.call-update) | async-done | bytes 1048592 | tf_op jit(solution)/shard_map/all_gather | solution.py:74
  963.7 5.9 multiply_reduce_fusion.2
  969.6 5.9 psum.45
  975.5 0.1 multiply_reduce_fusion.1
  975.6 5.7 psum.46
  981.3 0.8 multiply_add_fusion
  982.1 18.2 %all-gather.15.cloned.1.call-done = f32[2048,128]{1,0:T(8,128)} async-done(((f32[512,128]{1,0:T(8,128)}), f32[2048,128]{1,0:T(8,128)}) %all-gather.15.cloned.1.call-update) | async-done | bytes 1048592 | tf_op jit(solution)/shard_map/all_gather | solution.py:74
  1000.3 6.1 fusion.8
  1006.4 5.9 psum.47
  1012.3 1.0 add_convert_fusion
  1013.3 7.3 all_gather.39
  1020.6 2.6 convolution_convert_fusion
  1023.2 13.3 %all_to_all.16 = bf16[8,80,128]{2,1,0:T(8,128)(2,1)S(1)} all-to-all(bf16[8,80,128]{2,1,0:T(8,128)(2,1)S(1)} %bitcast.34), channel_id=1, replica_groups=mesh['tm'=8,'feat'=4] {'tm'}, dimensions={0} | all-to-all | bytes 327680 | tf_op jit(solution)/shard_map/all_to_all | solution.py:90
  1036.5 4.3 scatter_custom_fusion
  1040.8 0.2 multiply_reduce_fusion
  1040.9 0.6 broadcast_multiply_fusion.1
  (24 shorter events, 0.1 us)
Async XLA Ops:
  7.2 5.4 copy-start
  7.2 151.2 %all-gather.9.cloned.1.call-start = ((), (), s32[]{:S(2)}) async-start(), calls=%async_computation.3 | async-start | bytes 13107200 | tf_op jit(solution)/shard_map/all_gather | solution.py:49
  18.7 66.8 %copy-start.2 = (bf16[640,128]{1,0:T(8,128)(2,1)S(1)}, bf16[640,128]{1,0:T(8,128)(2,1)}, u32[]{:S(2)}) copy-start(bf16[640,128]{1,0:T(8,128)(2,1)} %param.6) | copy-start | bytes 491524
  88.3 11.2 %all-to-all-start.1 = ((bf16[8,80,128]{2,1,0:T(8,128)(2,1)}), bf16[8,80,128]{2,1,0:T(8,128)(2,1)S(1)}, u32[]{:S(2)}, u32[]{:S(2)}) async-start(bf16[8,80,128]{2,1,0:T(8,128)(2,1)} %broadcast_select_fusion.1), calls=%async_computation.1 | async-start | bytes 327680 | tf_op jit(solution)/shard_map/all_to_all | solution.py:44
  91.9 119.3 %all-gather.19.cloned.1.call-start = ((), (), s32[]{:S(2)}) async-start(), calls=%async_computation.8 | async-start | bytes 2359296 | tf_op jit(solution)/shard_map/all_gather | solution.py:15
  161.7 687.2 %all-gather.17.cloned.1.call-start = ((), (), s32[]{:S(2)}) async-start(), calls=%async_computation.7 | async-start | bytes 37748736 | tf_op jit(solution)/shard_map/all_gather | solution.py:15
  172.3 755.2 %all-gather.11.cloned.1.call-start = ((), (), s32[]{:S(2)}) async-start(), calls=%async_computation.4 | async-start | bytes 1310720 | tf_op jit(solution)/shard_map/all_gather | solution.py:74
  910.7 53.0 %all-gather.13.cloned.1.call-start = ((), (), s32[]{:S(2)}) async-start(), calls=%async_computation.5 | async-start | bytes 1310720 | tf_op jit(solution)/shard_map/all_gather | solution.py:74
  945.5 35.8 %copy-start.3 = (f32[512,128]{1,0:T(8,128)S(1)}, f32[512,128]{1,0:T(8,128)}, u32[]{:S(2)}) copy-start(f32[512,128]{1,0:T(8,128)} %multiply_add_fusion.1) | copy-start | bytes 786436
  945.5 54.8 %all-gather.15.cloned.1.call-start = ((), (), s32[]{:S(2)}) async-start(), calls=%async_computation.6 | async-start | bytes 1310720 | tf_op jit(solution)/shard_map/all_gather | solution.py:74
  1000.3 41.3 %copy-start.1 = (bf16[640,2048]{1,0:T(8,128)(2,1)S(1)}, bf16[640,2048]{1,0:T(8,128)(2,1)}, u32[]{:S(2)}) copy-start(bf16[640,2048]{1,0:T(8,128)(2,1)} %param.5) | copy-start | bytes 7864324
  1040.8 0.8 copy-start.4
Sparse Core Ops, SparseCore 0:
  85.6 72.7 all-gather.8
  161.9 49.2 all-gather.18
  212.7 636.2 all-gather.16
  910.8 16.6 all-gather.10
  945.6 18.0 all-gather.12
  982.2 18.0 all-gather.14
where the time goes:
time: 1050 us
  waiting for transfers between devices  784 us (75%)
  blocking collectives  128 us (12%)
  other arithmetic  73.1 us (7%)
  matrix products  34 us (3%)
  between operations  14.3 us (1%)
  local copies, waits for them, and re-layouts  10.5 us (1%)
    all_gather x2, waiting for transfers between devices, carried_in(): everything = jax.tree.map(lambda part: lax.all_gather(part, axis), shard)  677 us
    all_to_all x1, blocking collectives, body(): lax.all_to_all(sorted_x, 'tm', split_axis=0, concat_axis=0, tiled=True)  66.8 us
    select_n x16, other arithmetic, hop(): return jax.tree.map(lambda a, b: jnp.where(reached, a, b), new, before)  60.7 us
    all_gather x3, waiting for transfers between devices, body(): lax.all_gather(direction, 'feat', axis=0, tiled=True)  53 us
    all_gather x1, waiting for transfers between devices, body(): rows_x = lax.all_gather(local_x, 'feat', axis=0, tiled=True)  47.1 us
    psum x5, blocking collectives, column_dot(): return lax.psum(jnp.sum(left * right, axis=0), 'feat')  29 us
  transfers between devices with their start and end apart: 7, of which 7 were waited for; matrix products, arithmetic and copies ran while one was open for 1% of the time, Pallas kernels for 0%

commit v1 on v0

v1 whole, which is shorter than its diff:
```python
import jax
import jax.numpy as jnp
from jax import lax
from jax.sharding import PartitionSpec as P

ITERS = 3
RIDGE = 0.1
TINY = 1e-06
AXES = ("tm", "feat")


def body(activations, targets, span_of):
    spans = lax.axis_size("tm")
    feat_count = lax.axis_size("feat")
    devices = spans * feat_count
    tok_dev, width = activations.shape
    n_targets = targets.shape[1]
    rows = spans * n_targets
    own = rows // devices
    place = lax.axis_index("tm") * feat_count + lax.axis_index("feat")

    span_ids = jnp.arange(spans, dtype=jnp.int32)
    earlier = (span_of[:, None] < span_ids[None, :])[:, :, None]
    here = (span_of[:, None] == span_ids[None, :])[:, :, None]

    def back(masked):
        part = lax.dot_general(
            masked.reshape(tok_dev, rows),
            activations,
            (((0,), (0,)), ((), ())),
            preferred_element_type=jnp.float32,
        )
        return lax.psum_scatter(part, AXES, scatter_dimension=0, tiled=True)

    row_span = (place * own + jnp.arange(own, dtype=jnp.int32)) // n_targets
    seen = (row_span * (tok_dev * feat_count)).astype(jnp.float32)
    scale = (1.0 / jnp.maximum(seen, 1.0))[:, None]

    zero = jnp.zeros((), targets.dtype)
    rhs = scale * back(jnp.where(earlier, targets[:, None, :], zero))
    residual = rhs
    direction = rhs
    norm_now = jnp.sum(rhs * rhs, axis=1, keepdims=True)
    alphas = []
    kept = []
    for step in range(ITERS):
        sent = direction.astype(jnp.bfloat16)
        direction = sent.astype(jnp.float32)
        everywhere = lax.all_gather(sent, AXES, axis=0, tiled=True)
        image_t = lax.dot_general(
            activations,
            everywhere,
            (((1,), (1,)), ((), ())),
            preferred_element_type=jnp.float32,
        ).reshape(tok_dev, spans, n_targets)
        kept.append(jnp.sum(jnp.where(here, image_t, 0.0), axis=1))
        if step + 1 < ITERS:
            masked = jnp.where(earlier, image_t, 0.0).astype(jnp.bfloat16)
            image = scale * back(masked) + RIDGE * direction
            alpha = norm_now / (jnp.sum(direction * image, axis=1, keepdims=True) + TINY)
            alphas.append(alpha)
            residual = residual - alpha * image
            norm_next = jnp.sum(residual * residual, axis=1, keepdims=True)
            direction = residual + norm_next / (norm_now + TINY) * direction
            norm_now = norm_next
        else:
            squared = jnp.sum(jnp.where(earlier, image_t * image_t, 0.0), axis=0)
            squared = lax.psum(squared, AXES)
            ridge_part = RIDGE * jnp.sum(direction * direction, axis=1, keepdims=True)
            small = jnp.concatenate(alphas + [norm_now, ridge_part], axis=1).T
            small = lax.all_gather(small, AXES, axis=1, tiled=True)
            small = small.reshape(ITERS + 1, spans, n_targets)
            all_seen = (span_ids * (tok_dev * feat_count)).astype(jnp.float32)
            all_scale = (1.0 / jnp.maximum(all_seen, 1.0))[:, None]
            last = small[ITERS - 1] / (all_scale * squared + small[ITERS] + TINY)
            steps = [small[i] for i in range(ITERS - 1)] + [last]
    predicted = 0.0
    for size, value in zip(steps, kept):
        mine = jnp.sum(jnp.where(here, size[None], 0.0), axis=1)
        predicted = predicted + mine * value
    predictions = predicted.astype(jnp.bfloat16)
    error = targets.astype(jnp.float32) - predictions.astype(jnp.float32)
    surprise = jnp.mean(error * error, axis=1)
    return (predictions, surprise)


def solution(mesh):
    return jax.shard_map(
        body,
        mesh=mesh,
        in_specs=(P(AXES, None), P(AXES, None), P(AXES)),
        out_specs=(P(AXES, None), P(AXES)),
        check_vma=False,
    )
```

time: 1050 us -> 732 us (0.70)
  waiting for transfers between devices: 784 us -> 586 us
  other arithmetic: 73.1 us -> 14.9 us
  blocking collectives: 128 us -> 76 us
    all_gather x6 -> x3, waiting for transfers between devices: 777 us -> 139 us  [body(): everywhere = lax.all_gather(sent, AXES, axis=0, tiled=True)]
    reduce_scatter x0 -> x3, waiting for transfers between devices: none -> 447 us  [back(): return lax.psum_scatter(part, AXES, scatter_dimension=0, tiled=True)]
    all_to_all x2 -> x0, blocking collectives: 80 us -> none  [the longest x1 66.8 us: body(): lax.all_to_all(sorted_x, 'tm', split_axis=0, concat_axis=0, tiled=True)]
    select_n x19 -> x1, other arithmetic: 63.6 us -> 0.14 us  [body(): rhs = scale * back(jnp.where(earlier, targets[:, None, :], zero))]
    all_gather x2 -> x1, blocking collectives: 19.2 us -> 36.9 us  [body(): small = lax.all_gather(small, AXES, axis=1, tiled=True)]
    reduce_sum x2 -> x6, other arithmetic: 0.18 us -> 10.8 us  [the longest x1 4.14 us: body(): kept.append(jnp.sum(jnp.where(here, image_t, 0.0), axis=1))]
    psum x5 -> x1, blocking collectives: 29 us -> 39.1 us  [body(): squared = lax.psum(squared, AXES)]
  transfers between devices with their start and end apart: 7 -> 6, of which waited for: 7 -> 6; matrix products, arithmetic and copies ran while one was open for 1% -> 0% of each run, Pallas kernels for 0% -> 0%
where the time goes in v1:
time: 732 us
  waiting for transfers between devices  586 us (80%)
  blocking collectives  76 us (10%)
  matrix products  38.4 us (5%)
  other arithmetic  14.9 us (2%)
  between operations  14.2 us (2%)
    reduce_scatter x3, waiting for transfers between devices, back(): return lax.psum_scatter(part, AXES, scatter_dimension=0, tiled=True)  447 us
    all_gather x3, waiting for transfers between devices, body(): everywhere = lax.all_gather(sent, AXES, axis=0, tiled=True)  139 us
    psum x1, blocking collectives, body(): squared = lax.psum(squared, AXES)  39.1 us
    all_gather x1, blocking collectives, body(): small = lax.all_gather(small, AXES, axis=1, tiled=True)  36.9 us
    dot_general x3, matrix products, body(): lax.dot_general(activations, everywhere, (((1,), (1,)), ((), ())), prefer...  21.7 us
    dot_general x3, matrix products, back(): lax.dot_general(masked.reshape(tok_dev, rows), activations, (((0,), (0,))...  16.7 us
  transfers between devices with their start and end apart: 6, of which 6 were waited for; matrix products, arithmetic and copies ran while one was open for 0% of the time, Pallas kernels for 0%

profile of v1, /device:TPU:0, one launch (start us, length us, event | category | flops | bytes accessed | tf_op | source)
XLA Modules:
  0.0 731.8 jit_solution(4828201645293953744)
XLA Ops:
  7.2 0.0 copy-start
  7.2 0.0 reduce-scatter.4.cloned.1.call-start
  7.2 1.2 copy.8
  8.4 0.7 iota_compare_fusion.1
  9.1 0.1 bitcast_select_fusion.3
  9.3 0.0 copy-done
  9.3 5.6 fusion.13
  14.9 0.0 reduce-scatter.4.cloned.1.call-update
  14.9 0.0 all-gather.5.cloned.1.call-start
  15.0 151.7 %reduce-scatter.4.cloned.1.call-done = f32[32,2048]{1,0:T(8,128)} async-done(((f32[1024,2048]{1,0:T(8,128)}), f32[32,2048]{1,0:T(8,128)}) %reduce-scatter.4.cloned.1.call-update) | async-done | bytes 262160 | tf_op jit(solution)/shard_map/reduce_scatter | solution.py:33
  166.7 1.7 multiply_convert_fusion
  168.4 0.0 all-gather.5.cloned.1.call-update
  168.4 0.0 reduce-scatter.6.cloned.1.call-start
  168.4 59.7 %all-gather.5.cloned.1.call-done = bf16[1024,2048]{1,0:T(8,128)(2,1)} async-done(((bf16[32,2048]{1,0:T(8,128)(2,1)}), bf16[1024,2048]{1,0:T(8,128)(2,1)}) %all-gather.5.cloned.1.call-update) | async-done | bytes 4194320 | tf_op jit(solution)/shard_map/all_gather | solution.py:49
  228.1 7.2 fusion
  235.3 5.6 fusion.14
  240.9 0.0 copy-start.1
  240.9 0.0 reduce-scatter.6.cloned.1.call-update
  240.9 0.0 all-gather.7.cloned.1.call-start
  240.9 147.4 %reduce-scatter.6.cloned.1.call-done = f32[32,2048]{1,0:T(8,128)} async-done(((f32[1024,2048]{1,0:T(8,128)}), f32[32,2048]{1,0:T(8,128)}) %reduce-scatter.6.cloned.1.call-update) | async-done | bytes 262160 | tf_op jit(solution)/shard_map/reduce_scatter | solution.py:33
  388.3 0.0 copy-done.1
  388.3 1.2 fusion.4
  389.5 1.2 multiply_reduce_fusion.3
  390.7 0.8 fusion.6
  391.5 0.0 all-gather.7.cloned.1.call-update
  391.5 0.0 reduce-scatter.8.cloned.1.call-start
  391.6 58.3 %all-gather.7.cloned.1.call-done = bf16[1024,2048]{1,0:T(8,128)(2,1)} async-done(((bf16[32,2048]{1,0:T(8,128)(2,1)}), bf16[1024,2048]{1,0:T(8,128)(2,1)}) %all-gather.7.cloned.1.call-update) | async-done | bytes 4194320 | tf_op jit(solution)/shard_map/all_gather | solution.py:49
  449.9 7.2 fusion.1
  457.1 5.6 fusion.15
  462.7 0.0 copy-start.2
  462.7 0.0 reduce-scatter.8.cloned.1.call-update
  462.7 0.0 all-gather.9.cloned.1.call-start
  462.7 147.7 %reduce-scatter.8.cloned.1.call-done = f32[32,2048]{1,0:T(8,128)} async-done(((f32[1024,2048]{1,0:T(8,128)}), f32[32,2048]{1,0:T(8,128)}) %reduce-scatter.8.cloned.1.call-update) | async-done | bytes 262160 | tf_op jit(solution)/shard_map/reduce_scatter | solution.py:33
  610.4 0.0 copy-done.2
  610.4 1.2 fusion.8
  611.6 1.2 multiply_reduce_fusion.2
  612.8 1.9 multiply_reduce_fusion.1
  614.7 0.0 all-gather.9.cloned.1.call-update
  614.8 36.9 %all-gather = f32[32,32,4]{1,2,0:T(4,128)S(1)} all-gather(f32[1,32,4]{1,2,0:T(4,128)S(1)} %maximum_bitcast_fusion), channel_id=1, replica_groups=mesh['tm'=8,'feat'=4] {'tm','feat'}, dimensions={0}, use_global_device_ids=true | all-gather | bytes 16896 | tf_op jit(solution)/shard_map/all_gather | solution.py:71
  651.7 0.1 reshape.171
  651.8 21.1 %all-gather.9.cloned.1.call-done = bf16[1024,2048]{1,0:T(8,128)(2,1)} async-done(((bf16[32,2048]{1,0:T(8,128)(2,1)}), bf16[1024,2048]{1,0:T(8,128)(2,1)}) %all-gather.9.cloned.1.call-update) | async-done | bytes 4194320 | tf_op jit(solution)/shard_map/all_gather | solution.py:49
  672.8 7.3 fusion.2
  680.1 39.1 %psum.7 = f32[8,128]{1,0:T(8,128)S(1)} all-reduce(f32[8,128]{1,0:T(8,128)S(1)} %bitcast.63), channel_id=1, replica_groups=mesh['tm'=8,'feat'=4] {'tm','feat'}, use_global_device_ids=true, to_apply=%region_14.15 | all-reduce | flops 1024 | bytes 8192 | tf_op jit(solution)/shard_map/psum | solution.py:68
  719.2 0.1 add_divide_fusion
  719.3 4.1 select_reduce_fusion.4
  723.5 0.1 multiply_reduce_fusion
  723.6 0.8 copy.11
  724.4 0.6 broadcast_multiply_fusion
  (10 shorter events, 0.1 us)
Async XLA Ops:
  7.2 2.1 copy-start
  7.2 159.5 %reduce-scatter.4.cloned.1.call-start = ((), (), s32[]{:S(2)}) async-start(), calls=%async_computation.3 | async-start | bytes 8650752 | tf_op jit(solution)/shard_map/reduce_scatter | solution.py:33
  14.9 213.2 %all-gather.5.cloned.1.call-start = ((), (), s32[]{:S(2)}) async-start(), calls=%async_computation.4 | async-start | bytes 4325376 | tf_op jit(solution)/shard_map/all_gather | solution.py:49
  168.4 219.9 %reduce-scatter.6.cloned.1.call-start = ((), (), s32[]{:S(2)}) async-start(), calls=%async_computation.5 | async-start | bytes 8650752 | tf_op jit(solution)/shard_map/reduce_scatter | solution.py:33
  240.9 147.5 %copy-start.1 = (f32[32,2048]{1,0:T(8,128)S(1)}, f32[32,2048]{1,0:T(8,128)}, u32[]{:S(2)}) copy-start(f32[32,2048]{1,0:T(8,128)} %reduce-scatter.4.cloned.1.call-done) | copy-start | bytes 786436
  240.9 209.0 %all-gather.7.cloned.1.call-start = ((), (), s32[]{:S(2)}) async-start(), calls=%async_computation.6 | async-start | bytes 4325376 | tf_op jit(solution)/shard_map/all_gather | solution.py:49
  391.5 218.9 %reduce-scatter.8.cloned.1.call-start = ((), (), s32[]{:S(2)}) async-start(), calls=%async_computation.7 | async-start | bytes 8650752 | tf_op jit(solution)/shard_map/reduce_scatter | solution.py:33
  462.7 147.8 %copy-start.2 = (bf16[32,2048]{1,0:T(8,128)(2,1)S(1)}, bf16[32,2048]{1,0:T(8,128)(2,1)}, u32[]{:S(2)}) copy-start(bf16[32,2048]{1,0:T(8,128)(2,1)} %fusion.6) | copy-start | bytes 393220
  462.7 210.1 %all-gather.9.cloned.1.call-start = ((), (), s32[]{:S(2)}) async-start(), calls=%async_computation.8 | async-start | bytes 4325376 | tf_op jit(solution)/shard_map/all_gather | solution.py:49
Sparse Core Ops, SparseCore 0:
  15.0 151.5 reduce-scatter.3
  170.1 57.9 all-gather.4
  241.0 147.2 reduce-scatter.5
  391.6 58.1 all-gather.6
  462.8 147.5 reduce-scatter.7
  614.9 57.9 all-gather.8

commit v2 on v1

--- a/solution.py
+++ b/solution.py
@@ -30,7 +30,12 @@
             (((0,), (0,)), ((), ())),
             preferred_element_type=jnp.float32,
         )
-        return lax.psum_scatter(part, AXES, scatter_dimension=0, tiled=True)
+        part = part.reshape(spans, feat_count * own, width)
+        part = lax.psum_scatter(part, "feat", scatter_dimension=1, tiled=True)
+        pieces = lax.all_to_all(
+            part.astype(jnp.bfloat16), "tm", split_axis=0, concat_axis=0, tiled=True
+        )
+        return jnp.sum(pieces.astype(jnp.float32), axis=0)
 
     row_span = (place * own + jnp.arange(own, dtype=jnp.int32)) // n_targets
     seen = (row_span * (tok_dev * feat_count)).astype(jnp.float32)

time: 732 us -> 601 us (0.82)
  waiting for transfers between devices: 586 us -> 383 us
  blocking collectives: 76 us -> 140 us
    reduce_scatter x3, waiting for transfers between devices: 447 us -> 215 us  [back(): part = lax.psum_scatter(part, 'feat', scatter_dimension=1, tiled=True)]
    all_to_all x0 -> x2, blocking collectives: none -> 62.2 us  [back(): lax.all_to_all(part.astype(jnp.bfloat16), 'tm', split_axis=0, concat_axis...]
    all_to_all x0 -> x1, waiting for transfers between devices: none -> 25.8 us  [back(): lax.all_to_all(part.astype(jnp.bfloat16), 'tm', split_axis=0, concat_axis...]
  transfers between devices with their start and end apart: 6 -> 7, of which waited for: 6 -> 7; matrix products, arithmetic and copies ran while one was open for 0% -> 0% of each run, Pallas kernels for 0% -> 0%
where the time goes in v2:
time: 601 us
  waiting for transfers between devices  383 us (64%)
  blocking collectives  140 us (23%)
  matrix products  38.4 us (6%)
  other arithmetic  17.1 us (3%)
  between operations  14.2 us (2%)
    reduce_scatter x3, waiting for transfers between devices, back(): part = lax.psum_scatter(part, 'feat', scatter_dimension=1, tiled=True)  215 us
    all_gather x3, waiting for transfers between devices, body(): everywhere = lax.all_gather(sent, AXES, axis=0, tiled=True)  142 us
    all_to_all x2, blocking collectives, back(): lax.all_to_all(part.astype(jnp.bfloat16), 'tm', split_axis=0, concat_axis...  62.2 us
    all_gather x1, blocking collectives, body(): small = lax.all_gather(small, AXES, axis=1, tiled=True)  39.2 us
    psum x1, blocking collectives, body(): squared = lax.psum(squared, AXES)  39.1 us
    all_to_all x1, waiting for transfers between devices, back(): lax.all_to_all(part.astype(jnp.bfloat16), 'tm', split_axis=0, concat_axis...  25.8 us
    dot_general x3, matrix products, body(): lax.dot_general(activations, everywhere, (((1,), (1,)), ((), ())), prefer...  21.7 us
    dot_general x3, matrix products, back(): lax.dot_general(masked.reshape(tok_dev, rows), activations, (((0,), (0,))...  16.7 us
  transfers between devices with their start and end apart: 7, of which 7 were waited for; matrix products, arithmetic and copies ran while one was open for 0% of the time, Pallas kernels for 0%

profile of v2, /device:TPU:0, one launch (start us, length us, event | category | flops | bytes accessed | tf_op | source)
XLA Modules:
  0.0 600.9 jit_solution(10619375403940726177)
XLA Ops:
  7.2 0.0 copy-start
  7.2 0.0 reduce-scatter.4.cloned.1.call-start
  7.2 1.2 copy.12
  8.4 0.7 iota_compare_fusion.1
  9.1 0.1 bitcast_select_fusion.3
  9.3 0.0 copy-done
  9.3 5.6 fusion.7
  14.9 0.0 reduce-scatter.4.cloned.1.call-update
  14.9 74.6 %reduce-scatter.4.cloned.1.call-done = f32[8,32,2048]{2,1,0:T(8,128)} async-done(((f32[8,128,2048]{2,1,0:T(8,128)}), f32[8,32,2048]{2,1,0:T(8,128)}) %reduce-scatter.4.cloned.1.call-update) | async-done | bytes 2097168 | tf_op jit(solution)/shard_map/reduce_scatter | solution.py:34
  89.5 2.7 convert_element_type.68
  92.2 5.5 all-to-all-start
  97.8 0.0 all-gather.5.cloned.1.call-start
  97.8 25.8 %all-to-all-done = bf16[8,32,2048]{2,1,0:T(8,128)(2,1)} async-done(((bf16[8,32,2048]{2,1,0:T(8,128)(2,1)}), bf16[8,32,2048]{2,1,0:T(8,128)(2,1)}, u32[]{:S(2)}, u32[]{:S(2)}) %all-to-all-start) | async-done | bytes 1048608 | tf_op jit(solution)/shard_map/all_to_all | solution.py:35
  123.6 1.4 convert_reduce_fusion.2
  125.0 0.7 multiply_convert_fusion
  125.7 0.0 all-gather.5.cloned.1.call-update
  125.8 0.0 reduce-scatter.6.cloned.1.call-start
  125.8 60.2 %all-gather.5.cloned.1.call-done = bf16[1024,2048]{1,0:T(8,128)(2,1)} async-done(((bf16[32,2048]{1,0:T(8,128)(2,1)}), bf16[1024,2048]{1,0:T(8,128)(2,1)}) %all-gather.5.cloned.1.call-update) | async-done | bytes 4194320 | tf_op jit(solution)/shard_map/all_gather | solution.py:54
  186.1 7.2 %fusion = (bf16[640,1024]{0,1:T(8,128)(2,1)S(1)}, f32[1024,640]{1,0:T(8,128)}) fusion(pred[640,8]{0,1:T(8,128)(4,1)S(1)} %get-tuple-element.25, bf16[1024,2048]{1,0:T(8,128)(2,1)} %all-gather.5.cloned.1.call-done, bf16[640,2048]{1,0:T(8,128)(2,1)S(1)} %copy-done), kind=kOutput, calls=%fused_computation.4 | convolution fusion | flops 2685009920 | bytes 10753024 | tf_op jit(solution)/shard_map/dot_general | solution.py:55
  193.3 5.6 fusion.5
  198.8 0.0 reduce-scatter.6.cloned.1.call-update
  198.8 0.0 all-gather.7.cloned.1.call-start
  198.9 70.4 %reduce-scatter.6.cloned.1.call-done = f32[8,32,2048]{2,1,0:T(8,128)} async-done(((f32[8,128,2048]{2,1,0:T(8,128)}), f32[8,32,2048]{2,1,0:T(8,128)}) %reduce-scatter.6.cloned.1.call-update) | async-done | bytes 2097168 | tf_op jit(solution)/shard_map/reduce_scatter | solution.py:34
  269.3 1.7 convert_element_type.73
  271.0 31.1 %all_to_all.15 = bf16[8,32,2048]{2,1,0:T(8,128)(2,1)S(1)} all-to-all(bf16[8,32,2048]{2,1,0:T(8,128)(2,1)S(1)} %convert_element_type.73), channel_id=1, replica_groups=mesh['tm'=8,'feat'=4] {'tm'}, dimensions={0} | all-to-all | bytes 2097152 | tf_op jit(solution)/shard_map/all_to_all | solution.py:35
  302.1 0.1 convert_reduce_fusion.1
  302.2 0.3 fusion.10
  302.5 0.2 multiply_reduce_fusion.3
  302.7 0.8 fusion.12
  303.5 0.0 all-gather.7.cloned.1.call-update
  303.5 0.0 reduce-scatter.8.cloned.1.call-start
  303.6 60.2 %all-gather.7.cloned.1.call-done = bf16[1024,2048]{1,0:T(8,128)(2,1)} async-done(((bf16[32,2048]{1,0:T(8,128)(2,1)}), bf16[1024,2048]{1,0:T(8,128)(2,1)}) %all-gather.7.cloned.1.call-update) | async-done | bytes 4194320 | tf_op jit(solution)/shard_map/all_gather | solution.py:54
  363.8 7.2 %fusion.1 = (bf16[640,1024]{0,1:T(8,128)(2,1)S(1)}, f32[1024,640]{1,0:T(8,128)}) fusion(pred[640,8]{0,1:T(8,128)(4,1)S(1)} %get-tuple-element.25, bf16[1024,2048]{1,0:T(8,128)(2,1)} %all-gather.7.cloned.1.call-done, bf16[640,2048]{1,0:T(8,128)(2,1)S(1)} %copy-done), kind=kOutput, calls=%fused_computation.5 | convolution fusion | flops 2685009920 | bytes 10753024 | tf_op jit(solution)/shard_map/dot_general | solution.py:55
  371.0 5.6 fusion.3
  376.6 0.0 reduce-scatter.8.cloned.1.call-update
  376.6 0.0 copy-start.1
  376.6 0.0 all-gather.9.cloned.1.call-start
  376.7 70.4 %reduce-scatter.8.cloned.1.call-done = f32[8,32,2048]{2,1,0:T(8,128)} async-done(((f32[8,128,2048]{2,1,0:T(8,128)}), f32[8,32,2048]{2,1,0:T(8,128)}) %reduce-scatter.8.cloned.1.call-update) | async-done | bytes 2097168 | tf_op jit(solution)/shard_map/reduce_scatter | solution.py:34
  447.0 1.7 convert_element_type.78
  448.8 31.1 %all_to_all.16 = bf16[8,32,2048]{2,1,0:T(8,128)(2,1)S(1)} all-to-all(bf16[8,32,2048]{2,1,0:T(8,128)(2,1)S(1)} %convert_element_type.78), channel_id=1, replica_groups=mesh['tm'=8,'feat'=4] {'tm'}, dimensions={0} | all-to-all | bytes 2097152 | tf_op jit(solution)/shard_map/all_to_all | solution.py:35
  479.9 0.1 convert_reduce_fusion
  480.0 0.0 copy-done.1
  480.0 0.2 fusion.14
  480.3 0.2 multiply_reduce_fusion.2
  480.5 0.9 multiply_reduce_fusion.1
  481.4 0.0 all-gather.9.cloned.1.call-update
  481.5 39.2 %all-gather = f32[32,32,4]{1,2,0:T(4,128)S(1)} all-gather(f32[1,32,4]{1,2,0:T(4,128)S(1)} %maximum_bitcast_fusion), channel_id=1, replica_groups=mesh['tm'=8,'feat'=4] {'tm','feat'}, dimensions={0}, use_global_device_ids=true | all-gather | bytes 16896 | tf_op jit(solution)/shard_map/all_gather | solution.py:76
  520.7 0.1 reshape.177
  520.8 21.1 %all-gather.9.cloned.1.call-done = bf16[1024,2048]{1,0:T(8,128)(2,1)} async-done(((bf16[32,2048]{1,0:T(8,128)(2,1)}), bf16[1024,2048]{1,0:T(8,128)(2,1)}) %all-gather.9.cloned.1.call-update) | async-done | bytes 4194320 | tf_op jit(solution)/shard_map/all_gather | solution.py:54
  541.9 7.3 %fusion.2 = (f32[1024]{0:T(1024)S(1)}, f32[1024,640]{1,0:T(8,128)}) fusion(pred[640,8]{0,1:T(8,128)(4,1)S(1)} %get-tuple-element.25, bf16[1024,2048]{1,0:T(8,128)(2,1)} %all-gather.9.cloned.1.call-done, bf16[640,2048]{1,0:T(8,128)(2,1)S(1)} %copy-done), kind=kOutput, calls=%fused_computation.6 | convolution fusion | flops 2686319616 | bytes 9446400 | tf_op jit(solution)/shard_map/dot_general | solution.py:55
  549.1 39.1 %psum.7 = f32[8,128]{1,0:T(8,128)S(1)} all-reduce(f32[8,128]{1,0:T(8,128)S(1)} %bitcast.79), channel_id=1, replica_groups=mesh['tm'=8,'feat'=4] {'tm','feat'}, use_global_device_ids=true, to_apply=%region_17.18 | all-reduce | flops 1024 | bytes 8192 | tf_op jit(solution)/shard_map/psum | solution.py:73
  588.3 0.1 add_divide_fusion
  588.3 4.1 select_reduce_fusion.4
  592.5 0.1 multiply_reduce_fusion
  592.6 0.8 copy.15
  593.4 0.6 broadcast_multiply_fusion
  (10 shorter events, 0.1 us)
Async XLA Ops:
  7.2 2.1 copy-start
  7.2 82.3 %reduce-scatter.4.cloned.1.call-start = ((), (), s32[]{:S(2)}) async-start(), calls=%async_computation.6 | async-start | bytes 10485760 | tf_op jit(solution)/shard_map/reduce_scatter | solution.py:34
  92.2 31.4 %all-to-all-start = ((bf16[8,32,2048]{2,1,0:T(8,128)(2,1)}), bf16[8,32,2048]{2,1,0:T(8,128)(2,1)}, u32[]{:S(2)}, u32[]{:S(2)}) async-start(bf16[8,32,2048]{2,1,0:T(8,128)(2,1)} %convert_element_type.68), calls=%async_computation.1 | async-start | bytes 2097152 | tf_op jit(solution)/shard_map/all_to_all | solution.py:35
  97.8 88.3 %all-gather.5.cloned.1.call-start = ((), (), s32[]{:S(2)}) async-start(), calls=%async_computation.7 | async-start | bytes 4325376 | tf_op jit(solution)/shard_map/all_gather | solution.py:54
  125.8 143.5 %reduce-scatter.6.cloned.1.call-start = ((), (), s32[]{:S(2)}) async-start(), calls=%async_computation.8 | async-start | bytes 10485760 | tf_op jit(solution)/shard_map/reduce_scatter | solution.py:34
  198.8 165.0 %all-gather.7.cloned.1.call-start = ((), (), s32[]{:S(2)}) async-start(), calls=%async_computation.9 | async-start | bytes 4325376 | tf_op jit(solution)/shard_map/all_gather | solution.py:54
  303.5 143.5 %reduce-scatter.8.cloned.1.call-start = ((), (), s32[]{:S(2)}) async-start(), calls=%async_computation.10 | async-start | bytes 10485760 | tf_op jit(solution)/shard_map/reduce_scatter | solution.py:34
  376.6 103.4 %copy-start.1 = (bf16[32,2048]{1,0:T(8,128)(2,1)S(1)}, bf16[32,2048]{1,0:T(8,128)(2,1)}, u32[]{:S(2)}) copy-start(bf16[32,2048]{1,0:T(8,128)(2,1)} %fusion.12) | copy-start | bytes 393220
  376.6 165.2 %all-gather.9.cloned.1.call-start = ((), (), s32[]{:S(2)}) async-start(), calls=%async_computation.11 | async-start | bytes 4325376 | tf_op jit(solution)/shard_map/all_gather | solution.py:54
Sparse Core Ops, SparseCore 0:
  15.0 74.4 reduce-scatter.3
  125.9 60.1 all-gather.4
  199.0 70.2 reduce-scatter.5
  303.7 60.1 all-gather.6
  376.7 70.2 reduce-scatter.7
  481.6 60.2 all-gather.8
